TPU v7x, 32 devices: a whole 2x2x4 slice. The times are simulated.
32 devices in a mesh: tm: 4 (over y, x), pix: 8 (over z, core).
Axes of the slice: x: 2, y: 2, z: 4, core: 2. Of those that a mesh axis runs over, the one named last changes fastest.
Arguments:
- latent: float32 [16, 32, 448], P(None, 'pix'), may hold values from -6 to 6
- step_size: float32 [8], P('tm'), may hold values from 0.05 to 0.2
- time_embed: float32 [8, 128], P('tm'), may hold values from -6 to 6
- conv_in: bfloat16 [3, 3, 128, 16], replicated, may hold values from -0.5 to 0.5
- conv_mid: bfloat16 [3, 3, 128, 128], replicated, may hold values from -0.1875 to 0.1875
- conv_out: bfloat16 [3, 3, 16, 128], replicated, may hold values from -0.1875 to 0.1875
Outputs:
- trajectory: float32 [8, 16, 32, 448], P('tm', None, 'pix')
All inputs are finite; a program needn't handle non-finite values.
Results may differ from a plain program's by a relative error of at most 0.00075.
Values may be sent and summed in bfloat16 or wider, within the bound.
A program may use at most 64 MiB of HBM per device.

v0:
```python
import jax
import jax.numpy as jnp
from jax import lax
from jax.sharding import PartitionSpec as P

ITERS = 3


def with_halo(x, sides, width):
    for axis, dim in sides:
        peers, length = (lax.axis_size(axis), x.shape[dim])
        up = [(i, (i + 1) % peers) for i in range(peers - 1)]
        down = [(j, i) for i, j in up]
        last = lax.slice_in_dim(x, length - width, length, axis=dim)
        first = lax.slice_in_dim(x, 0, width, axis=dim)
        before = lax.ppermute(last, axis, up)
        after = lax.ppermute(first, axis, down)
        x = jnp.concatenate([before, x, after], axis=dim)
    return x


def convolve_rows(values, kernel):
    span_rows = values.shape[2] - 2
    span_cols = values.shape[3]
    padded = jnp.pad(values, ((0, 0), (0, 0), (0, 0), (1, 1)))
    summed = jnp.zeros((values.shape[0], kernel.shape[2], span_rows, span_cols), jnp.float32)
    for row_shift in range(3):
        for col_shift in range(3):
            summed = summed + jnp.einsum(
                "oi,tirw->torw",
                kernel[row_shift, col_shift],
                padded[:, :, row_shift : row_shift + span_rows, col_shift : col_shift + span_cols],
                preferred_element_type=jnp.float32,
            )
    return summed


def block_three(current, time_embed, conv_in, conv_mid, conv_out):
    lowered = current.astype(jnp.bfloat16)
    ext_in = with_halo(lowered, (("pix", 2),), 1)
    first_pre = convolve_rows(ext_in, conv_in) + time_embed[:, :, None, None]
    hidden = jax.nn.silu(first_pre).astype(jnp.bfloat16)
    ext_hidden = with_halo(hidden, (("pix", 2),), 1)
    second = jax.nn.silu(convolve_rows(ext_hidden, conv_mid)).astype(jnp.bfloat16)
    ext_second = with_halo(second, (("pix", 2),), 1)
    return current + convolve_rows(ext_second, conv_out)


def prefix_gathered(section_total):
    my_index = lax.axis_index("tm")
    shard_rows = lax.all_gather(section_total[None], "tm", axis=0, tiled=True)
    positions = jnp.arange(shard_rows.shape[0], dtype=jnp.int32)
    lower = (positions < my_index).astype(jnp.float32)
    return jnp.sum(shard_rows * lower[:, None, None, None], axis=0)


def shards(latent, step_size, time_embed, conv_in, conv_mid, conv_out):
    count = step_size.shape[0]
    states = jnp.broadcast_to(latent[None], (count,) + latent.shape)
    trajectory = states
    for rounds in range(ITERS):
        outputs = block_three(states, time_embed, conv_in, conv_mid, conv_out)
        drifts = step_size[:, None, None, None] * outputs
        local_sum = jnp.cumsum(drifts, axis=0)
        section_total = local_sum[-1]
        before = prefix_gathered(section_total)
        trajectory = latent[None] + (before[None] + local_sum)
        states = jnp.concatenate([(latent + before)[None], trajectory[:-1]], axis=0)
    return trajectory


def solution(mesh):
    in_specs = (P(None, "pix", None), P("tm"), P("tm", None), P(), P(), P())
    out_specs = P("tm", None, "pix", None)
    return jax.shard_map(shards, mesh=mesh, in_specs=in_specs, out_specs=out_specs, check_vma=False)
```

profile of v0, /device:TPU:15, one launch (start us, length us, event | category | flops | bytes accessed | tf_op | source)
XLA Modules:
  0.0 155.1 jit_solution(8705566869574266016)
XLA Ops:
  0.0 1.0 copy.52
  1.0 2.6 %collective-permute-start.1 = (bf16[2,16,1,448]{3,1,2,0:T(8,128)(2,1)S(1)}, bf16[2,16,1,448]{3,1,2,0:T(8,128)(2,1)S(1)}, u32[]{:S(2)}, u32[]{:S(2)}) collective-permute-start(bf16[2,16,1,448]{3,1,2,0:T(8,128)(2,1)S(1)} %add.395), channel_id=1, source_target_pairs={{1,0},{2,1},{3,2},{4,3},{5,4},{6,5},{7,6},{9,8},{10,9},{11,10},{12... | collective-permute-start | bytes 86024 | tf_op jit(solution)/shard_map/ppermute | solution.py:17
  3.6 3.1 %collective-permute-start = (bf16[2,16,1,448]{3,1,2,0:T(8,128)(2,1)S(1)}, bf16[2,16,1,448]{3,1,2,0:T(8,128)(2,1)S(1)}, u32[]{:S(2)}, u32[]{:S(2)}) collective-permute-start(bf16[2,16,1,448]{3,1,2,0:T(8,128)(2,1)S(1)} %add.393), channel_id=1, source_target_pairs={{0,1},{1,2},{2,3},{3,4},{4,5},{5,6},{6,7},{8,9},{9,10},{10,11},{11... | collective-permute-start | bytes 86024 | tf_op jit(solution)/shard_map/ppermute | solution.py:16
  6.8 1.1 fusion.248
  8.6 0.7 fusion.240
  9.7 0.7 fusion.244
  11.8 1.2 fusion.22
  13.0 4.0 %collective-permute-start.2 = (bf16[2,128,1,448]{1,3,2,0:T(8,128)(2,1)S(1)}, bf16[2,128,1,448]{1,3,2,0:T(8,128)(2,1)S(1)}, u32[]{:S(2)}, u32[]{:S(2)}) collective-permute-start(bf16[2,128,1,448]{1,3,2,0:T(8,128)(2,1)S(1)} %get-tuple-element.15), channel_id=1, source_target_pairs={{0,1},{1,2},{2,3},{3,4},{4,5},{5,6},{6,7},{8,9},{9,10},{10,11},{11... | collective-permute-start | bytes 688136 | tf_op jit(solution)/shard_map/ppermute | solution.py:16
  17.0 1.9 %collective-permute-start.3 = (bf16[2,128,1,448]{1,3,2,0:T(8,128)(2,1)S(1)}, bf16[2,128,1,448]{1,3,2,0:T(8,128)(2,1)S(1)}, u32[]{:S(2)}, u32[]{:S(2)}) collective-permute-start(bf16[2,128,1,448]{1,3,2,0:T(8,128)(2,1)S(1)} %get-tuple-element.16), channel_id=1, source_target_pairs={{1,0},{2,1},{3,2},{4,3},{5,4},{6,5},{7,6},{9,8},{10,9},{11,10},{12... | collective-permute-start | bytes 688136 | tf_op jit(solution)/shard_map/ppermute | solution.py:17
  19.4 0.6 collective-permute-done.2
  20.0 4.4 %collective-permute-done.3 = bf16[2,128,1,448]{1,3,2,0:T(8,128)(2,1)S(1)} collective-permute-done((bf16[2,128,1,448]{1,3,2,0:T(8,128)(2,1)S(1)}, bf16[2,128,1,448]{1,3,2,0:T(8,128)(2,1)S(1)}, u32[]{:S(2)}, u32[]{:S(2)}) %collective-permute-start.3) | collective-permute-done | bytes 229408 | tf_op jit(solution)/shard_map/ppermute | solution.py:17
  27.6 1.2 fusion.19
  28.8 1.9 %collective-permute-start.4 = (bf16[2,128,1,448]{1,3,2,0:T(8,128)(2,1)S(1)}, bf16[2,128,1,448]{1,3,2,0:T(8,128)(2,1)S(1)}, u32[]{:S(2)}, u32[]{:S(2)}) collective-permute-start(bf16[2,128,1,448]{1,3,2,0:T(8,128)(2,1)S(1)} %get-tuple-element.13), channel_id=1, source_target_pairs={{0,1},{1,2},{2,3},{3,4},{4,5},{5,6},{6,7},{8,9},{9,10},{10,11},{11... | collective-permute-start | bytes 688136 | tf_op jit(solution)/shard_map/ppermute | solution.py:16
  30.7 2.4 %collective-permute-start.5 = (bf16[2,128,1,448]{1,3,2,0:T(8,128)(2,1)S(1)}, bf16[2,128,1,448]{1,3,2,0:T(8,128)(2,1)S(1)}, u32[]{:S(2)}, u32[]{:S(2)}) collective-permute-start(bf16[2,128,1,448]{1,3,2,0:T(8,128)(2,1)S(1)} %get-tuple-element.14), channel_id=1, source_target_pairs={{1,0},{2,1},{3,2},{4,3},{5,4},{6,5},{7,6},{9,8},{10,9},{11,10},{12... | collective-permute-start | bytes 688136 | tf_op jit(solution)/shard_map/ppermute | solution.py:17
  33.6 4.4 %collective-permute-done.5 = bf16[2,128,1,448]{1,3,2,0:T(8,128)(2,1)S(1)} collective-permute-done((bf16[2,128,1,448]{1,3,2,0:T(8,128)(2,1)S(1)}, bf16[2,128,1,448]{1,3,2,0:T(8,128)(2,1)S(1)}, u32[]{:S(2)}, u32[]{:S(2)}) %collective-permute-start.5) | collective-permute-done | bytes 229408 | tf_op jit(solution)/shard_map/ppermute | solution.py:17
  42.3 0.9 fusion.446
  43.2 8.7 %all_gather.9 = f32[4,16,4,448]{3,1,2,0:T(8,128)S(1)} all-gather(f32[1,16,4,448]{3,1,2,0:T(8,128)S(1)} %slice.628), channel_id=1, replica_groups=mesh['tm'=4,'pix'=8] {'tm'}, dimensions={0}, use_global_device_ids=true | all-gather | bytes 573440 | tf_op jit(solution)/shard_map/all_gather | solution.py:51
  52.2 3.5 %collective-permute-start.6 = (bf16[2,16,1,448]{3,1,2,0:T(8,128)(2,1)S(1)}, bf16[2,16,1,448]{3,1,2,0:T(8,128)(2,1)S(1)}, u32[]{:S(2)}, u32[]{:S(2)}) collective-permute-start(bf16[2,16,1,448]{3,1,2,0:T(8,128)(2,1)S(1)} %get-tuple-element.19), channel_id=1, source_target_pairs={{0,1},{1,2},{2,3},{3,4},{4,5},{5,6},{6,7},{8,9},{9,10},{10,11},{11... | collective-permute-start | bytes 86024 | tf_op jit(solution)/shard_map/ppermute | solution.py:16
  55.7 2.1 %collective-permute-start.7 = (bf16[2,16,1,448]{3,1,2,0:T(8,128)(2,1)S(1)}, bf16[2,16,1,448]{3,1,2,0:T(8,128)(2,1)S(1)}, u32[]{:S(2)}, u32[]{:S(2)}) collective-permute-start(bf16[2,16,1,448]{3,1,2,0:T(8,128)(2,1)S(1)} %get-tuple-element.20), channel_id=1, source_target_pairs={{1,0},{2,1},{3,2},{4,3},{5,4},{6,5},{7,6},{9,8},{10,9},{11,10},{12... | collective-permute-start | bytes 86024 | tf_op jit(solution)/shard_map/ppermute | solution.py:17
  58.2 2.7 %collective-permute-done.7 = bf16[2,16,1,448]{3,1,2,0:T(8,128)(2,1)S(1)} collective-permute-done((bf16[2,16,1,448]{3,1,2,0:T(8,128)(2,1)S(1)}, bf16[2,16,1,448]{3,1,2,0:T(8,128)(2,1)S(1)}, u32[]{:S(2)}, u32[]{:S(2)}) %collective-permute-start.7) | collective-permute-done | bytes 28704 | tf_op jit(solution)/shard_map/ppermute | solution.py:17
  61.5 0.7 fusion.225
  62.6 0.7 fusion.229
  64.7 1.2 fusion.23
  65.9 1.9 %collective-permute-start.8 = (bf16[2,128,1,448]{1,3,2,0:T(8,128)(2,1)S(1)}, bf16[2,128,1,448]{1,3,2,0:T(8,128)(2,1)S(1)}, u32[]{:S(2)}, u32[]{:S(2)}) collective-permute-start(bf16[2,128,1,448]{1,3,2,0:T(8,128)(2,1)S(1)} %get-tuple-element.11), channel_id=1, source_target_pairs={{0,1},{1,2},{2,3},{3,4},{4,5},{5,6},{6,7},{8,9},{9,10},{10,11},{11... | collective-permute-start | bytes 688136 | tf_op jit(solution)/shard_map/ppermute | solution.py:16
  67.8 2.4 %collective-permute-start.9 = (bf16[2,128,1,448]{1,3,2,0:T(8,128)(2,1)S(1)}, bf16[2,128,1,448]{1,3,2,0:T(8,128)(2,1)S(1)}, u32[]{:S(2)}, u32[]{:S(2)}) collective-permute-start(bf16[2,128,1,448]{1,3,2,0:T(8,128)(2,1)S(1)} %get-tuple-element.12), channel_id=1, source_target_pairs={{1,0},{2,1},{3,2},{4,3},{5,4},{6,5},{7,6},{9,8},{10,9},{11,10},{12... | collective-permute-start | bytes 688136 | tf_op jit(solution)/shard_map/ppermute | solution.py:17
  70.8 4.4 %collective-permute-done.9 = bf16[2,128,1,448]{1,3,2,0:T(8,128)(2,1)S(1)} collective-permute-done((bf16[2,128,1,448]{1,3,2,0:T(8,128)(2,1)S(1)}, bf16[2,128,1,448]{1,3,2,0:T(8,128)(2,1)S(1)}, u32[]{:S(2)}, u32[]{:S(2)}) %collective-permute-start.9) | collective-permute-done | bytes 229408 | tf_op jit(solution)/shard_map/ppermute | solution.py:17
  78.4 1.2 fusion.20
  79.6 1.9 %collective-permute-start.10 = (bf16[2,128,1,448]{1,3,2,0:T(8,128)(2,1)S(1)}, bf16[2,128,1,448]{1,3,2,0:T(8,128)(2,1)S(1)}, u32[]{:S(2)}, u32[]{:S(2)}) collective-permute-start(bf16[2,128,1,448]{1,3,2,0:T(8,128)(2,1)S(1)} %get-tuple-element.9), channel_id=1, source_target_pairs={{0,1},{1,2},{2,3},{3,4},{4,5},{5,6},{6,7},{8,9},{9,10},{10,11},{11... | collective-permute-start | bytes 688136 | tf_op jit(solution)/shard_map/ppermute | solution.py:16
  81.5 2.4 %collective-permute-start.11 = (bf16[2,128,1,448]{1,3,2,0:T(8,128)(2,1)S(1)}, bf16[2,128,1,448]{1,3,2,0:T(8,128)(2,1)S(1)}, u32[]{:S(2)}, u32[]{:S(2)}) collective-permute-start(bf16[2,128,1,448]{1,3,2,0:T(8,128)(2,1)S(1)} %get-tuple-element.10), channel_id=1, source_target_pairs={{1,0},{2,1},{3,2},{4,3},{5,4},{6,5},{7,6},{9,8},{10,9},{11,10},{12... | collective-permute-start | bytes 688136 | tf_op jit(solution)/shard_map/ppermute | solution.py:17
  84.4 4.4 %collective-permute-done.11 = bf16[2,128,1,448]{1,3,2,0:T(8,128)(2,1)S(1)} collective-permute-done((bf16[2,128,1,448]{1,3,2,0:T(8,128)(2,1)S(1)}, bf16[2,128,1,448]{1,3,2,0:T(8,128)(2,1)S(1)}, u32[]{:S(2)}, u32[]{:S(2)}) %collective-permute-start.11) | collective-permute-done | bytes 229408 | tf_op jit(solution)/shard_map/ppermute | solution.py:17
  93.0 0.9 fusion.447
  94.0 9.7 %all_gather.10 = f32[4,16,4,448]{3,1,2,0:T(8,128)S(1)} all-gather(f32[1,16,4,448]{3,1,2,0:T(8,128)S(1)} %slice.654), channel_id=1, replica_groups=mesh['tm'=4,'pix'=8] {'tm'}, dimensions={0}, use_global_device_ids=true | all-gather | bytes 573440 | tf_op jit(solution)/shard_map/all_gather | solution.py:51
  103.9 2.7 %collective-permute-start.12 = (bf16[2,16,1,448]{3,1,2,0:T(8,128)(2,1)S(1)}, bf16[2,16,1,448]{3,1,2,0:T(8,128)(2,1)S(1)}, u32[]{:S(2)}, u32[]{:S(2)}) collective-permute-start(bf16[2,16,1,448]{3,1,2,0:T(8,128)(2,1)S(1)} %get-tuple-element.17), channel_id=1, source_target_pairs={{0,1},{1,2},{2,3},{3,4},{4,5},{5,6},{6,7},{8,9},{9,10},{10,11},{11... | collective-permute-start | bytes 86024 | tf_op jit(solution)/shard_map/ppermute | solution.py:16
  106.7 2.1 %collective-permute-start.13 = (bf16[2,16,1,448]{3,1,2,0:T(8,128)(2,1)S(1)}, bf16[2,16,1,448]{3,1,2,0:T(8,128)(2,1)S(1)}, u32[]{:S(2)}, u32[]{:S(2)}) collective-permute-start(bf16[2,16,1,448]{3,1,2,0:T(8,128)(2,1)S(1)} %get-tuple-element.18), channel_id=1, source_target_pairs={{1,0},{2,1},{3,2},{4,3},{5,4},{6,5},{7,6},{9,8},{10,9},{11,10},{12... | collective-permute-start | bytes 86024 | tf_op jit(solution)/shard_map/ppermute | solution.py:17
  109.3 2.6 %collective-permute-done.13 = bf16[2,16,1,448]{3,1,2,0:T(8,128)(2,1)S(1)} collective-permute-done((bf16[2,16,1,448]{3,1,2,0:T(8,128)(2,1)S(1)}, bf16[2,16,1,448]{3,1,2,0:T(8,128)(2,1)S(1)}, u32[]{:S(2)}, u32[]{:S(2)}) %collective-permute-start.13) | collective-permute-done | bytes 28704 | tf_op jit(solution)/shard_map/ppermute | solution.py:17
  112.5 0.7 fusion.210
  113.6 0.7 fusion.214
  115.6 1.2 fusion.24
  116.9 1.9 %collective-permute-start.14 = (bf16[2,128,1,448]{1,3,2,0:T(8,128)(2,1)S(1)}, bf16[2,128,1,448]{1,3,2,0:T(8,128)(2,1)S(1)}, u32[]{:S(2)}, u32[]{:S(2)}) collective-permute-start(bf16[2,128,1,448]{1,3,2,0:T(8,128)(2,1)S(1)} %get-tuple-element.7), channel_id=1, source_target_pairs={{0,1},{1,2},{2,3},{3,4},{4,5},{5,6},{6,7},{8,9},{9,10},{10,11},{11... | collective-permute-start | bytes 688136 | tf_op jit(solution)/shard_map/ppermute | solution.py:16
  118.8 2.4 %collective-permute-start.15 = (bf16[2,128,1,448]{1,3,2,0:T(8,128)(2,1)S(1)}, bf16[2,128,1,448]{1,3,2,0:T(8,128)(2,1)S(1)}, u32[]{:S(2)}, u32[]{:S(2)}) collective-permute-start(bf16[2,128,1,448]{1,3,2,0:T(8,128)(2,1)S(1)} %get-tuple-element.8), channel_id=1, source_target_pairs={{1,0},{2,1},{3,2},{4,3},{5,4},{6,5},{7,6},{9,8},{10,9},{11,10},{12... | collective-permute-start | bytes 688136 | tf_op jit(solution)/shard_map/ppermute | solution.py:17
  121.7 4.4 %collective-permute-done.15 = bf16[2,128,1,448]{1,3,2,0:T(8,128)(2,1)S(1)} collective-permute-done((bf16[2,128,1,448]{1,3,2,0:T(8,128)(2,1)S(1)}, bf16[2,128,1,448]{1,3,2,0:T(8,128)(2,1)S(1)}, u32[]{:S(2)}, u32[]{:S(2)}) %collective-permute-start.15) | collective-permute-done | bytes 229408 | tf_op jit(solution)/shard_map/ppermute | solution.py:17
  129.4 1.2 fusion.21
  130.6 1.9 %collective-permute-start.16 = (bf16[2,128,1,448]{1,3,2,0:T(8,128)(2,1)S(1)}, bf16[2,128,1,448]{1,3,2,0:T(8,128)(2,1)S(1)}, u32[]{:S(2)}, u32[]{:S(2)}) collective-permute-start(bf16[2,128,1,448]{1,3,2,0:T(8,128)(2,1)S(1)} %get-tuple-element.5), channel_id=1, source_target_pairs={{0,1},{1,2},{2,3},{3,4},{4,5},{5,6},{6,7},{8,9},{9,10},{10,11},{11... | collective-permute-start | bytes 688136 | tf_op jit(solution)/shard_map/ppermute | solution.py:16
  132.5 2.4 %collective-permute-start.17 = (bf16[2,128,1,448]{1,3,2,0:T(8,128)(2,1)S(1)}, bf16[2,128,1,448]{1,3,2,0:T(8,128)(2,1)S(1)}, u32[]{:S(2)}, u32[]{:S(2)}) collective-permute-start(bf16[2,128,1,448]{1,3,2,0:T(8,128)(2,1)S(1)} %get-tuple-element.6), channel_id=1, source_target_pairs={{1,0},{2,1},{3,2},{4,3},{5,4},{6,5},{7,6},{9,8},{10,9},{11,10},{12... | collective-permute-start | bytes 688136 | tf_op jit(solution)/shard_map/ppermute | solution.py:17
  135.5 4.4 %collective-permute-done.17 = bf16[2,128,1,448]{1,3,2,0:T(8,128)(2,1)S(1)} collective-permute-done((bf16[2,128,1,448]{1,3,2,0:T(8,128)(2,1)S(1)}, bf16[2,128,1,448]{1,3,2,0:T(8,128)(2,1)S(1)}, u32[]{:S(2)}, u32[]{:S(2)}) %collective-permute-start.17) | collective-permute-done | bytes 229408 | tf_op jit(solution)/shard_map/ppermute | solution.py:17
  144.1 0.9 fusion.448
  145.0 9.1 %all_gather.11 = f32[4,16,4,448]{3,1,2,0:T(8,128)S(1)} all-gather(f32[1,16,4,448]{3,1,2,0:T(8,128)S(1)} %slice.680), channel_id=1, replica_groups=mesh['tm'=4,'pix'=8] {'tm'}, dimensions={0}, use_global_device_ids=true | all-gather | bytes 573440 | tf_op jit(solution)/shard_map/all_gather | solution.py:51
  154.2 0.9 copy.21
  (125 shorter events, 34.1 us)
Async XLA Ops:
  0.0 7.9 %copy-start.1 = (f32[16,4,448]{2,1,0:T(4,128)S(1)}, f32[16,4,448]{2,1,0:T(4,128)}, u32[]{:S(2)}) copy-start(f32[16,4,448]{2,1,0:T(4,128)} %param.6) | copy-start | bytes 344068
  0.0 8.1 %copy-start.2 = (bf16[3,3,128,16]{2,3,1,0:T(8,128)(2,1)S(1)}, bf16[3,3,128,16]{2,3,1,0:T(8,128)(2,1)}, u32[]{:S(2)}) copy-start(bf16[3,3,128,16]{2,3,1,0:T(8,128)(2,1)} %param.9) | copy-start | bytes 110596
  1.0 6.9 %collective-permute-start.1 = (bf16[2,16,1,448]{3,1,2,0:T(8,128)(2,1)S(1)}, bf16[2,16,1,448]{3,1,2,0:T(8,128)(2,1)S(1)}, u32[]{:S(2)}, u32[]{:S(2)}) collective-permute-start(bf16[2,16,1,448]{3,1,2,0:T(8,128)(2,1)S(1)} %add.395), channel_id=1, source_target_pairs={{1,0},{2,1},{3,2},{4,3},{5,4},{6,5},{7,6},{9,8},{10,9},{11,10},{12... | collective-permute-start | bytes 86024 | tf_op jit(solution)/shard_map/ppermute | solution.py:17
  3.6 4.3 %collective-permute-start = (bf16[2,16,1,448]{3,1,2,0:T(8,128)(2,1)S(1)}, bf16[2,16,1,448]{3,1,2,0:T(8,128)(2,1)S(1)}, u32[]{:S(2)}, u32[]{:S(2)}) collective-permute-start(bf16[2,16,1,448]{3,1,2,0:T(8,128)(2,1)S(1)} %add.393), channel_id=1, source_target_pairs={{0,1},{1,2},{2,3},{3,4},{4,5},{5,6},{6,7},{8,9},{9,10},{10,11},{11... | collective-permute-start | bytes 86024 | tf_op jit(solution)/shard_map/ppermute | solution.py:16
  10.9 0.9 copy-start.4
  11.8 7.2 %copy-start = (bf16[3,3,128,128]{3,2,1,0:T(8,128)(2,1)S(1)}, bf16[3,3,128,128]{3,2,1,0:T(8,128)(2,1)}, u32[]{:S(2)}) copy-start(bf16[3,3,128,128]{3,2,1,0:T(8,128)(2,1)} %param.10) | copy-start | bytes 884740
  13.0 6.9 %collective-permute-start.2 = (bf16[2,128,1,448]{1,3,2,0:T(8,128)(2,1)S(1)}, bf16[2,128,1,448]{1,3,2,0:T(8,128)(2,1)S(1)}, u32[]{:S(2)}, u32[]{:S(2)}) collective-permute-start(bf16[2,128,1,448]{1,3,2,0:T(8,128)(2,1)S(1)} %get-tuple-element.15), channel_id=1, source_target_pairs={{0,1},{1,2},{2,3},{3,4},{4,5},{5,6},{6,7},{8,9},{9,10},{10,11},{11... | collective-permute-start | bytes 688136 | tf_op jit(solution)/shard_map/ppermute | solution.py:16
  17.0 7.3 %collective-permute-start.3 = (bf16[2,128,1,448]{1,3,2,0:T(8,128)(2,1)S(1)}, bf16[2,128,1,448]{1,3,2,0:T(8,128)(2,1)S(1)}, u32[]{:S(2)}, u32[]{:S(2)}) collective-permute-start(bf16[2,128,1,448]{1,3,2,0:T(8,128)(2,1)S(1)} %get-tuple-element.16), channel_id=1, source_target_pairs={{1,0},{2,1},{3,2},{4,3},{5,4},{6,5},{7,6},{9,8},{10,9},{11,10},{12... | collective-permute-start | bytes 688136 | tf_op jit(solution)/shard_map/ppermute | solution.py:17
  27.6 5.6 %copy-start.3 = (bf16[3,3,16,128]{3,2,1,0:T(8,128)(2,1)S(1)}, bf16[3,3,16,128]{3,2,1,0:T(8,128)(2,1)}, u32[]{:S(2)}) copy-start(bf16[3,3,16,128]{3,2,1,0:T(8,128)(2,1)} %param.11) | copy-start | bytes 110596
  28.8 4.9 %collective-permute-start.4 = (bf16[2,128,1,448]{1,3,2,0:T(8,128)(2,1)S(1)}, bf16[2,128,1,448]{1,3,2,0:T(8,128)(2,1)S(1)}, u32[]{:S(2)}, u32[]{:S(2)}) collective-permute-start(bf16[2,128,1,448]{1,3,2,0:T(8,128)(2,1)S(1)} %get-tuple-element.13), channel_id=1, source_target_pairs={{0,1},{1,2},{2,3},{3,4},{4,5},{5,6},{6,7},{8,9},{9,10},{10,11},{11... | collective-permute-start | bytes 688136 | tf_op jit(solution)/shard_map/ppermute | solution.py:16
  30.7 7.3 %collective-permute-start.5 = (bf16[2,128,1,448]{1,3,2,0:T(8,128)(2,1)S(1)}, bf16[2,128,1,448]{1,3,2,0:T(8,128)(2,1)S(1)}, u32[]{:S(2)}, u32[]{:S(2)}) collective-permute-start(bf16[2,128,1,448]{1,3,2,0:T(8,128)(2,1)S(1)} %get-tuple-element.14), channel_id=1, source_target_pairs={{1,0},{2,1},{3,2},{4,3},{5,4},{6,5},{7,6},{9,8},{10,9},{11,10},{12... | collective-permute-start | bytes 688136 | tf_op jit(solution)/shard_map/ppermute | solution.py:17
  40.8 1.0 copy-start.5
  52.2 6.1 %collective-permute-start.6 = (bf16[2,16,1,448]{3,1,2,0:T(8,128)(2,1)S(1)}, bf16[2,16,1,448]{3,1,2,0:T(8,128)(2,1)S(1)}, u32[]{:S(2)}, u32[]{:S(2)}) collective-permute-start(bf16[2,16,1,448]{3,1,2,0:T(8,128)(2,1)S(1)} %get-tuple-element.19), channel_id=1, source_target_pairs={{0,1},{1,2},{2,3},{3,4},{4,5},{5,6},{6,7},{8,9},{9,10},{10,11},{11... | collective-permute-start | bytes 86024 | tf_op jit(solution)/shard_map/ppermute | solution.py:16
  55.7 5.2 %collective-permute-start.7 = (bf16[2,16,1,448]{3,1,2,0:T(8,128)(2,1)S(1)}, bf16[2,16,1,448]{3,1,2,0:T(8,128)(2,1)S(1)}, u32[]{:S(2)}, u32[]{:S(2)}) collective-permute-start(bf16[2,16,1,448]{3,1,2,0:T(8,128)(2,1)S(1)} %get-tuple-element.20), channel_id=1, source_target_pairs={{1,0},{2,1},{3,2},{4,3},{5,4},{6,5},{7,6},{9,8},{10,9},{11,10},{12... | collective-permute-start | bytes 86024 | tf_op jit(solution)/shard_map/ppermute | solution.py:17
  65.9 4.9 %collective-permute-start.8 = (bf16[2,128,1,448]{1,3,2,0:T(8,128)(2,1)S(1)}, bf16[2,128,1,448]{1,3,2,0:T(8,128)(2,1)S(1)}, u32[]{:S(2)}, u32[]{:S(2)}) collective-permute-start(bf16[2,128,1,448]{1,3,2,0:T(8,128)(2,1)S(1)} %get-tuple-element.11), channel_id=1, source_target_pairs={{0,1},{1,2},{2,3},{3,4},{4,5},{5,6},{6,7},{8,9},{9,10},{10,11},{11... | collective-permute-start | bytes 688136 | tf_op jit(solution)/shard_map/ppermute | solution.py:16
  67.8 7.3 %collective-permute-start.9 = (bf16[2,128,1,448]{1,3,2,0:T(8,128)(2,1)S(1)}, bf16[2,128,1,448]{1,3,2,0:T(8,128)(2,1)S(1)}, u32[]{:S(2)}, u32[]{:S(2)}) collective-permute-start(bf16[2,128,1,448]{1,3,2,0:T(8,128)(2,1)S(1)} %get-tuple-element.12), channel_id=1, source_target_pairs={{1,0},{2,1},{3,2},{4,3},{5,4},{6,5},{7,6},{9,8},{10,9},{11,10},{12... | collective-permute-start | bytes 688136 | tf_op jit(solution)/shard_map/ppermute | solution.py:17
  79.6 4.9 %collective-permute-start.10 = (bf16[2,128,1,448]{1,3,2,0:T(8,128)(2,1)S(1)}, bf16[2,128,1,448]{1,3,2,0:T(8,128)(2,1)S(1)}, u32[]{:S(2)}, u32[]{:S(2)}) collective-permute-start(bf16[2,128,1,448]{1,3,2,0:T(8,128)(2,1)S(1)} %get-tuple-element.9), channel_id=1, source_target_pairs={{0,1},{1,2},{2,3},{3,4},{4,5},{5,6},{6,7},{8,9},{9,10},{10,11},{11... | collective-permute-start | bytes 688136 | tf_op jit(solution)/shard_map/ppermute | solution.py:16
  81.5 7.3 %collective-permute-start.11 = (bf16[2,128,1,448]{1,3,2,0:T(8,128)(2,1)S(1)}, bf16[2,128,1,448]{1,3,2,0:T(8,128)(2,1)S(1)}, u32[]{:S(2)}, u32[]{:S(2)}) collective-permute-start(bf16[2,128,1,448]{1,3,2,0:T(8,128)(2,1)S(1)} %get-tuple-element.10), channel_id=1, source_target_pairs={{1,0},{2,1},{3,2},{4,3},{5,4},{6,5},{7,6},{9,8},{10,9},{11,10},{12... | collective-permute-start | bytes 688136 | tf_op jit(solution)/shard_map/ppermute | solution.py:17
  103.9 5.3 %collective-permute-start.12 = (bf16[2,16,1,448]{3,1,2,0:T(8,128)(2,1)S(1)}, bf16[2,16,1,448]{3,1,2,0:T(8,128)(2,1)S(1)}, u32[]{:S(2)}, u32[]{:S(2)}) collective-permute-start(bf16[2,16,1,448]{3,1,2,0:T(8,128)(2,1)S(1)} %get-tuple-element.17), channel_id=1, source_target_pairs={{0,1},{1,2},{2,3},{3,4},{4,5},{5,6},{6,7},{8,9},{9,10},{10,11},{11... | collective-permute-start | bytes 86024 | tf_op jit(solution)/shard_map/ppermute | solution.py:16
  106.7 5.2 %collective-permute-start.13 = (bf16[2,16,1,448]{3,1,2,0:T(8,128)(2,1)S(1)}, bf16[2,16,1,448]{3,1,2,0:T(8,128)(2,1)S(1)}, u32[]{:S(2)}, u32[]{:S(2)}) collective-permute-start(bf16[2,16,1,448]{3,1,2,0:T(8,128)(2,1)S(1)} %get-tuple-element.18), channel_id=1, source_target_pairs={{1,0},{2,1},{3,2},{4,3},{5,4},{6,5},{7,6},{9,8},{10,9},{11,10},{12... | collective-permute-start | bytes 86024 | tf_op jit(solution)/shard_map/ppermute | solution.py:17
  116.9 4.9 %collective-permute-start.14 = (bf16[2,128,1,448]{1,3,2,0:T(8,128)(2,1)S(1)}, bf16[2,128,1,448]{1,3,2,0:T(8,128)(2,1)S(1)}, u32[]{:S(2)}, u32[]{:S(2)}) collective-permute-start(bf16[2,128,1,448]{1,3,2,0:T(8,128)(2,1)S(1)} %get-tuple-element.7), channel_id=1, source_target_pairs={{0,1},{1,2},{2,3},{3,4},{4,5},{5,6},{6,7},{8,9},{9,10},{10,11},{11... | collective-permute-start | bytes 688136 | tf_op jit(solution)/shard_map/ppermute | solution.py:16
  118.8 7.3 %collective-permute-start.15 = (bf16[2,128,1,448]{1,3,2,0:T(8,128)(2,1)S(1)}, bf16[2,128,1,448]{1,3,2,0:T(8,128)(2,1)S(1)}, u32[]{:S(2)}, u32[]{:S(2)}) collective-permute-start(bf16[2,128,1,448]{1,3,2,0:T(8,128)(2,1)S(1)} %get-tuple-element.8), channel_id=1, source_target_pairs={{1,0},{2,1},{3,2},{4,3},{5,4},{6,5},{7,6},{9,8},{10,9},{11,10},{12... | collective-permute-start | bytes 688136 | tf_op jit(solution)/shard_map/ppermute | solution.py:17
  130.6 4.9 %collective-permute-start.16 = (bf16[2,128,1,448]{1,3,2,0:T(8,128)(2,1)S(1)}, bf16[2,128,1,448]{1,3,2,0:T(8,128)(2,1)S(1)}, u32[]{:S(2)}, u32[]{:S(2)}) collective-permute-start(bf16[2,128,1,448]{1,3,2,0:T(8,128)(2,1)S(1)} %get-tuple-element.5), channel_id=1, source_target_pairs={{0,1},{1,2},{2,3},{3,4},{4,5},{5,6},{6,7},{8,9},{9,10},{10,11},{11... | collective-permute-start | bytes 688136 | tf_op jit(solution)/shard_map/ppermute | solution.py:16
  132.5 7.3 %collective-permute-start.17 = (bf16[2,128,1,448]{1,3,2,0:T(8,128)(2,1)S(1)}, bf16[2,128,1,448]{1,3,2,0:T(8,128)(2,1)S(1)}, u32[]{:S(2)}, u32[]{:S(2)}) collective-permute-start(bf16[2,128,1,448]{1,3,2,0:T(8,128)(2,1)S(1)} %get-tuple-element.6), channel_id=1, source_target_pairs={{1,0},{2,1},{3,2},{4,3},{5,4},{6,5},{7,6},{9,8},{10,9},{11,10},{12... | collective-permute-start | bytes 688136 | tf_op jit(solution)/shard_map/ppermute | solution.py:17
where the time goes:
time: 157 us; the launch traced here: 155 us
  starting transfers between devices  43.7 us (28%)
  matrix products  42.3 us (27%)
  waiting for transfers between devices  32.7 us (21%)
  blocking collectives  27.4 us (17%)
  other arithmetic  6 us (4%)
  local copies, waits for them, and re-layouts  2.22 us (1%)
    dot_general x81, matrix products, convolve_rows(): jnp.einsum('oi,tirw->torw', kernel[row_shift, col_shift], padded[:, :, ro...  42.3 us
    ppermute x9, waiting for transfers between devices, with_halo(): after = lax.ppermute(first, axis, down)  31.7 us
    all_gather x3, blocking collectives, prefix_gathered(): shard_rows = lax.all_gather(section_total[None], 'tm', axis=0, tiled=True)  27.4 us
    ppermute x9, starting transfers between devices, with_halo(): before = lax.ppermute(last, axis, up)  22.9 us
    ppermute x9, starting transfers between devices, with_halo(): after = lax.ppermute(first, axis, down)  20.8 us
  transfers between devices with their start and end apart: 18, of which 14 were waited for; matrix products, arithmetic and copies ran while one was open for 3% of the time, Pallas kernels for 0%

commit v1 on v0

v1 whole, which is shorter than its diff:
```python
import functools

import jax
import jax.numpy as jnp
from jax import lax
from jax.experimental import pallas as pl
from jax.experimental.pallas import tpu as pltpu
from jax.sharding import PartitionSpec as P

ITERS = 3
LANES = 128
MESH = pl.DeviceIdType.MESH


def kernel(
    sizes,
    step_ref, latent_ref, te_ref, cin_ref, cmid_ref, cout_ref,
    out_ref,
    win, wmid, wout, lat, low0, halo0, im, pre0, hid, ysum, mask,
    table, bias, own, stage, halo, final, landed,
    sem0_send, sem0_recv, tab_send, tab_recv, halo_send, halo_recv, fin_send, fin_recv,
):
    sections, peers, per, total, chan, feat, rows, width, cols, margin, lanes = sizes
    q, p = lax.axis_index("tm"), lax.axis_index("pix")
    evals = total - ITERS + 1
    edge = 3 * lanes
    hid_rows, sec_rows, low_rows = rows + 4, rows + 2, rows + 6

    barrier = pltpu.get_barrier_semaphore()
    for s in range(1, sections):
        pl.semaphore_signal(barrier, inc=1, device_id=(lax.rem(q + s, sections), p), device_id_type=MESH)

    @pl.when(p > 0)
    def _():
        pl.semaphore_signal(barrier, inc=1, device_id=(q, p - 1), device_id_type=MESH)

    @pl.when(p < peers - 1)
    def _():
        pl.semaphore_signal(barrier, inc=1, device_id=(q, p + 1), device_id_type=MESH)

    for j in range(per):
        table[q * per + j] = jnp.concatenate(
            [te_ref[j : j + 1, :], jnp.full((7, feat), step_ref[j], jnp.float32)], axis=0
        )

    padded = (width + 2 * margin + LANES - 1) // LANES * LANES
    for r in range(rows):
        line = jnp.concatenate(
            [latent_ref[:, r, :], jnp.zeros((chan, padded - width), jnp.float32)], axis=1
        )
        for b in range(3):
            shift = lax.rem(margin + 1 - b - q * cols + 2 * padded, padded)
            view = pltpu.roll(line, shift, 1)[:, :lanes]
            low0[b, :, r * lanes : (r + 1) * lanes] = view.astype(jnp.bfloat16)
            if b == 1:
                lat[:, r * lanes : (r + 1) * lanes] = view

    @pl.when(p == 0)
    def _():
        halo0[0] = jnp.zeros(halo0.shape[1:], jnp.bfloat16)
        halo[0] = jnp.zeros(halo.shape[1:], jnp.bfloat16)

    @pl.when(p == peers - 1)
    def _():
        halo0[1] = jnp.zeros(halo0.shape[1:], jnp.bfloat16)
        halo[1] = jnp.zeros(halo.shape[1:], jnp.bfloat16)

    def table_copy(s):
        mine = table.at[pl.ds(q * per, per)]
        return pltpu.make_async_remote_copy(
            src_ref=mine, dst_ref=mine, send_sem=tab_send.at[s - 1], recv_sem=tab_recv.at[s - 1],
            device_id=(lax.rem(q + s, sections), p), device_id_type=MESH,
        )

    def first_copy(up):
        src = low0.at[:, :, pl.ds(0 if up else (rows - 3) * lanes, edge)]
        return pltpu.make_async_remote_copy(
            src_ref=src, dst_ref=halo0.at[1 if up else 0],
            send_sem=sem0_send.at[1 if up else 0], recv_sem=sem0_recv.at[1 if up else 0],
            device_id=(q, p - 1 if up else p + 1), device_id_type=MESH,
        )

    def halo_copy(up, slot):
        src = stage.at[slot, :, pl.ds(0 if up else (rows - 3) * lanes, edge)]
        side = 1 if up else 0
        return pltpu.make_async_remote_copy(
            src_ref=src, dst_ref=halo.at[side, slot],
            send_sem=halo_send.at[side, slot], recv_sem=halo_recv.at[side, slot],
            device_id=(q, p - 1 if up else p + 1), device_id_type=MESH,
        )

    def final_copy(source, j):
        return pltpu.make_async_remote_copy(
            src_ref=source, dst_ref=landed.at[q, lax.rem(j, per)],
            send_sem=fin_send.at[j], recv_sem=fin_recv.at[q, lax.rem(j, per)],
            device_id=(lax.div(j, per), p), device_id_type=MESH,
        )

    def deliver(source, j):
        owner = lax.div(jnp.int32(j), jnp.int32(per))

        @pl.when(owner == q)
        def _():
            landed[q, lax.rem(j, per)] = source[...]

        @pl.when(owner != q)
        def _():
            final_copy(source, j).start()

    pl.semaphore_wait(
        barrier, sections - 1 + (p > 0).astype(jnp.int32) + (p < peers - 1).astype(jnp.int32)
    )

    @pl.when(p > 0)
    def _():
        first_copy(True).start()

    @pl.when(p < peers - 1)
    def _():
        first_copy(False).start()

    for s in range(1, sections):
        table_copy(s).start()

    for a in range(3):
        for b in range(3):
            t = 3 * a + b
            win[:, t * chan : (t + 1) * chan] = cin_ref[a, b]
            wmid[:, t * feat : (t + 1) * feat] = cmid_ref[a, b]
            wout[t * chan : (t + 1) * chan, :] = cout_ref[a, b]

    col = lax.broadcasted_iota(jnp.int32, (8, lanes), 1) + (q * cols - margin)
    inside = jnp.where((col >= 0) & (col < width), 0.5, 0.0).astype(jnp.float32)
    for h in range(hid_rows):
        row = p * rows - 2 + h
        valid = ((row >= 0) & (row < peers * rows)).astype(jnp.float32)
        mask[:, h * lanes : (h + 1) * lanes] = inside * valid

    def gated(v, m):
        h = v * m
        return h + h * jnp.tanh(h)

    def spread(lows):
        for a in range(3):
            for b in range(3):
                t = 3 * a + b
                im[t * chan : (t + 1) * chan, :] = lows[b][:, a * lanes : (a + hid_rows) * lanes]

    def first_layer(pre, j, h0, count):
        te = bias[j]
        for i in range(count):
            h = h0 + i
            v = pre[:, i * lanes : (i + 1) * lanes] + te
            x = gated(v, mask[0:1, h * lanes : (h + 1) * lanes])
            span = slice(h * lanes, (h + 1) * lanes)
            hid[0:feat, span] = pltpu.roll(x, 1, 1).astype(jnp.bfloat16)
            hid[feat : 2 * feat, span] = x.astype(jnp.bfloat16)
            hid[2 * feat :, span] = pltpu.roll(x, lanes - 1, 1).astype(jnp.bfloat16)

    def rest(j):
        w = wmid[...]
        for s0 in range(0, sec_rows, 2):
            n = min(2, sec_rows - s0)
            x = jnp.concatenate(
                [hid[:, (s0 + a) * lanes : (s0 + a + n) * lanes] for a in range(3)], axis=0
            )
            v = jnp.dot(w, x, preferred_element_type=jnp.float32)
            m = mask[0:1, (s0 + 1) * lanes : (s0 + 1 + n) * lanes]
            second = gated(v, m).astype(jnp.bfloat16)
            ysum[:, s0 * lanes : (s0 + n) * lanes] = jnp.dot(
                wout[...], second, preferred_element_type=jnp.float32
            )
        parts = []
        for b in range(3):
            z = None
            for a in range(3):
                t = 3 * a + b
                y = ysum[t * chan : (t + 1) * chan, a * lanes : (a + rows) * lanes]
                z = y if z is None else z + y
            parts.append(z)
        return parts[1] + pltpu.roll(parts[0], 1, 1) + pltpu.roll(parts[2], rows * lanes - 1, 1)

    @pl.when(p < peers - 1)
    def _():
        first_copy(True).wait_recv()

    @pl.when(p > 0)
    def _():
        first_copy(False).wait_recv()

    spread([jnp.concatenate([halo0[0, b], low0[b], halo0[1, b]], axis=1) for b in range(3)])
    for h0 in range(0, hid_rows, 2):
        n = min(2, hid_rows - h0)
        span = slice(h0 * lanes, (h0 + n) * lanes)
        pre0[:, span] = jnp.dot(win[...], im[:, span], preferred_element_type=jnp.float32)

    for s in range(1, sections):
        table_copy(s).wait_recv()
    for j in range(total):
        bias[j] = jnp.broadcast_to(table[j, 0:1, :], (feat, feat)).T

    flat = jnp.concatenate([inside[0:1, :] * 2.0] * rows, axis=1)

    def advance(k, j, summed):
        slot = k * evals + j - k
        if k == 0:
            state = lat[...]
            first_layer(pre0[...], j, 0, hid_rows)
        else:
            came = slot - evals

            @pl.when(p < peers - 1)
            def _():
                halo_copy(True, came).wait_recv()

            @pl.when(p > 0)
            def _():
                halo_copy(False, came).wait_recv()

            state = own[came]
            centre = jnp.concatenate(
                [halo[0, came].astype(jnp.float32), state, halo[1, came].astype(jnp.float32)], axis=1
            )
            span = low_rows * lanes
            spread([
                pltpu.roll(centre, 1, 1).astype(jnp.bfloat16),
                centre.astype(jnp.bfloat16),
                pltpu.roll(centre, span - 1, 1).astype(jnp.bfloat16),
            ])
            for h0 in range(0, hid_rows, 2):
                n = min(2, hid_rows - h0)
                pre = jnp.dot(
                    win[...], im[:, h0 * lanes : (h0 + n) * lanes], preferred_element_type=jnp.float32
                )
                first_layer(pre, j, h0, n)
        output = state + rest(j)
        step = table[j, 1:2, :]
        summed = summed + jnp.concatenate([step] * rows, axis=1) * output
        reached = lat[...] + summed
        if k < ITERS - 1:
            reached = reached * flat
            own[slot] = reached
            stage[slot] = reached.astype(jnp.bfloat16)

            @pl.when(p > 0)
            def _():
                halo_copy(True, slot).start()

            @pl.when(p < peers - 1)
            def _():
                halo_copy(False, slot).start()
        else:
            final[j] = reached
            deliver(final.at[j], j)
        return summed

    start = jnp.zeros((chan, rows * lanes), jnp.float32)
    for k in range(ITERS):
        first = advance(k, jnp.int32(k), start)
        if k < ITERS - 1:
            deliver(own.at[k * evals], k)

        def body(j, summed, k=k):
            return advance(k, j, summed)

        lax.fori_loop(k + 1, k + evals, body, first)
        start = first

    for s in range(1, sections):
        table_copy(s).wait_send()

    @pl.when(p > 0)
    def _():
        first_copy(True).wait_send()

    @pl.when(p < peers - 1)
    def _():
        first_copy(False).wait_send()

    def drain(slot, carry):
        @pl.when(p > 0)
        def _():
            halo_copy(True, slot).wait_send()

        @pl.when(p < peers - 1)
        def _():
            halo_copy(False, slot).wait_send()

        return carry

    lax.fori_loop(0, (ITERS - 1) * evals, drain, 0)

    for j in range(total):
        @pl.when(jnp.int32(j // per) != q)
        def _(j=j):
            final_copy(final.at[j], jnp.int32(j)).wait_send()

    for s in range(sections):
        @pl.when(q != s)
        def _(s=s):
            for j in range(per):
                pltpu.make_async_remote_copy(
                    src_ref=landed.at[s, j], dst_ref=landed.at[s, j],
                    send_sem=fin_send.at[j], recv_sem=fin_recv.at[s, j],
                    device_id=(jnp.int32(s), p), device_id_type=MESH,
                ).wait_recv()

    for s in range(sections):
        for j in range(per):
            block = landed[s, j]
            for r in range(rows):
                out_ref[j, r, :, s * cols : (s + 1) * cols] = block[
                    :, r * lanes + margin : r * lanes + margin + cols
                ]


def shards(latent, step_size, time_embed, conv_in, conv_mid, conv_out):
    sections, peers = lax.axis_size("tm"), lax.axis_size("pix")
    chan, rows, width = latent.shape
    per, feat = time_embed.shape
    total = sections * per
    cols = width // sections
    margin = 3 * ITERS - 1
    lanes = (cols + 2 * margin + LANES - 1) // LANES * LANES
    evals = total - ITERS + 1
    slots = (ITERS - 1) * evals
    sizes = (sections, peers, per, total, chan, feat, rows, width, cols, margin, lanes)
    vmem = pl.BlockSpec(memory_space=pltpu.VMEM)
    f32, bf16 = jnp.float32, jnp.bfloat16
    dma = pltpu.SemaphoreType.DMA
    out = pl.pallas_call(
        functools.partial(kernel, sizes),
        out_shape=jax.ShapeDtypeStruct((per, rows, chan, width), f32),
        in_specs=[pl.BlockSpec(memory_space=pltpu.SMEM)] + [vmem] * 5,
        out_specs=vmem,
        scratch_shapes=[
            pltpu.VMEM((feat, 9 * chan), bf16),
            pltpu.VMEM((feat, 9 * feat), bf16),
            pltpu.VMEM((9 * chan, feat), bf16),
            pltpu.VMEM((chan, rows * lanes), f32),
            pltpu.VMEM((3, chan, rows * lanes), bf16),
            pltpu.VMEM((2, 3, chan, 3 * lanes), bf16),
            pltpu.VMEM((9 * chan, (rows + 4) * lanes), bf16),
            pltpu.VMEM((feat, (rows + 4) * lanes), f32),
            pltpu.VMEM((3 * feat, (rows + 4) * lanes), bf16),
            pltpu.VMEM((9 * chan, (rows + 2) * lanes), f32),
            pltpu.VMEM((8, (rows + 4) * lanes), f32),
            pltpu.VMEM((total, 8, feat), f32),
            pltpu.VMEM((total, feat, feat), f32),
            pltpu.VMEM((slots, chan, rows * lanes), f32),
            pltpu.VMEM((slots, chan, rows * lanes), bf16),
            pltpu.VMEM((2, slots, chan, 3 * lanes), bf16),
            pltpu.VMEM((total, chan, rows * lanes), f32),
            pltpu.VMEM((sections, per, chan, rows * lanes), f32),
            dma((2,)), dma((2,)),
            dma((sections - 1,)), dma((sections - 1,)),
            dma((2, slots)), dma((2, slots)),
            dma((total,)), dma((sections, per)),
        ],
        compiler_params=pltpu.CompilerParams(
            collective_id=0, has_side_effects=True, vmem_limit_bytes=40 * 1024 * 1024
        ),
    )(step_size, latent, time_embed, conv_in, conv_mid, conv_out)
    return jnp.transpose(out, (0, 2, 1, 3))


def solution(mesh):
    in_specs = (P(None, "pix", None), P("tm"), P("tm", None), P(), P(), P())
    out_specs = P("tm", None, "pix", None)
    return jax.shard_map(shards, mesh=mesh, in_specs=in_specs, out_specs=out_specs, check_vma=False)
```

time: 157 us -> 39.1 us (0.25)
  starting transfers between devices: 43.7 us -> 0 us
  matrix products: 42.3 us -> 0 us
  Pallas kernels: 0 us -> 34.4 us
  waiting for transfers between devices: 32.7 us -> 0 us
  blocking collectives: 27.4 us -> 0 us
  other arithmetic: 6 us -> 0 us
  local copies, waits for them, and re-layouts: 2.22 us -> 4.14 us
    ppermute x18 -> x0, starting transfers between devices: 43.7 us -> none  [the longest x9 22.9 us: with_halo(): before = lax.ppermute(last, axis, up)]
    dot_general x81 -> x0, matrix products: 42.3 us -> none  [convolve_rows(): jnp.einsum('oi,tirw->torw', kernel[row_shift, col_shift], padded[:, :, ro...]
    pallas_call x0 -> x1, Pallas kernels: none -> 34.4 us  [shards(): pl.pallas_call(functools.partial(kernel, sizes), out_shape=jax.ShapeDtype...]
    ppermute x18 -> x0, waiting for transfers between devices: 32.7 us -> none  [the longest x9 31.7 us: with_halo(): after = lax.ppermute(first, axis, down)]
    all_gather x3 -> x0, blocking collectives: 27.4 us -> none  [prefix_gathered(): shard_rows = lax.all_gather(section_total[None], 'tm', axis=0, tiled=True)]
    another operation x3 -> x0, other arithmetic: 2.79 us -> none  [shards(): local_sum = jnp.cumsum(drifts, axis=0)]
    concatenate x9 -> x0, other arithmetic: 2.62 us -> none  [with_halo(): x = jnp.concatenate([before, x, after], axis=dim)]
    unnamed x14 -> x11, local copies, waits for them, and re-layouts: 1.09 us -> 3.27 us
  transfers between devices with their start and end apart: 18 -> 0, of which waited for: 14 -> 0; matrix products, arithmetic and copies ran while one was open for 3% -> 0% of each run, Pallas kernels for 0% -> 0%
where the time goes in v1:
time: 39.1 us; the launch traced here: 38.6 us
  Pallas kernels  34.4 us (88%)
  local copies, waits for them, and re-layouts  4.14 us (11%)
    pallas_call x1, Pallas kernels, shards(): pl.pallas_call(functools.partial(kernel, sizes), out_shape=jax.ShapeDtype...  34.4 us
    unnamed x11, local copies, waits for them, and re-layouts  3.27 us
    transpose x1, local copies, waits for them, and re-layouts, shards(): return jnp.transpose(out, (0, 2, 1, 3))  0.87 us

profile of v1, /device:TPU:15, one launch (start us, length us, event | category | flops | bytes accessed | tf_op | source)
XLA Modules:
  0.0 38.6 jit_solution(2374161019145272068)
XLA Ops:
  0.0 0.0 copy-start.2
  0.0 0.0 copy-start
  0.0 1.0 %copy.7.cin_ref = bf16[3,3,128,16]{3,2,1,0:T(8,128)(2,1)S(1)} copy(bf16[3,3,128,16]{2,3,1,0:T(8,128)(2,1)} %param.9) | data formatting | bytes 73728 | tf_op args[3]
  1.0 0.0 copy-done.2
  1.0 0.0 copy-done
  1.1 0.0 copy-start.1
  1.1 0.9 %copy-done.1 = f32[16,4,448]{2,1,0:T(4,128)S(1)} copy-done((f32[16,4,448]{2,1,0:T(4,128)S(1)}, f32[16,4,448]{2,1,0:T(4,128)}, u32[]{:S(2)}) %copy-start.1) | copy-done | bytes 114712
  2.0 0.0 copy-start.3
  2.0 0.7 %copy-done.3 = f32[2,128]{1,0:T(2,128)S(1)} copy-done((f32[2,128]{1,0:T(2,128)S(1)}, f32[2,128]{1,0:T(2,128)}, u32[]{:S(2)}) %copy-start.3) | copy-done | bytes 1048
  2.6 0.0 copy-start.4
  2.6 0.7 %copy-done.4 = f32[2]{0:T(128)S(1)} copy-done((f32[2]{0:T(128)S(1)}, f32[2]{0:T(128)}, u32[]{:S(2)}) %copy-start.4) | copy-done | bytes 32
  3.3 34.4 %shard_map.64 = f32[2,4,16,448]{3,2,1,0:T(8,128)S(1)} custom-call(f32[2]{0:T(128)S(1)} %copy-done.4, f32[16,4,448]{2,1,0:T(4,128)S(1)} %copy-done.1, f32[2,128]{1,0:T(2,128)S(1)} %copy-done.3, bf16[3,3,128,16]{3,2,1,0:T(8,128)(2,1)S(1)} %copy.7.cin_ref, bf16[3,3,128,128]{3,2,1,0:T(8,128)(2,1)S(1)} %copy-done, bf16[3,3,16,128]{3,2,1,0:T(8,128)(2,1)S(1)} %copy-done.2), custom_call_target="tpu_custom_call" | custom-call | tf_op jit(solution)/shard_map/pallas_call | solution.py:331
  37.7 0.9 %copy.8 = f32[2,16,4,448]{3,2,1,0:T(4,128)} copy(f32[2,16,4,448]{3,1,2,0:T(8,128)S(1)} %bitcast.1) | data formatting | bytes 458752 | tf_op jit(solution)/shard_map/transpose | solution.py:364
Async XLA Ops:
  0.0 1.0 %copy-start.2 = (bf16[3,3,16,128]{3,2,1,0:T(8,128)(2,1)S(1)}, bf16[3,3,16,128]{3,2,1,0:T(8,128)(2,1)}, u32[]{:S(2)}) copy-start(bf16[3,3,16,128]{3,2,1,0:T(8,128)(2,1)} %cout_ref.1) | copy-start | bytes 110596
  0.0 1.0 %copy-start = (bf16[3,3,128,128]{3,2,1,0:T(8,128)(2,1)S(1)}, bf16[3,3,128,128]{3,2,1,0:T(8,128)(2,1)}, u32[]{:S(2)}) copy-start(bf16[3,3,128,128]{3,2,1,0:T(8,128)(2,1)} %cmid_ref.1) | copy-start | bytes 884740
  1.1 0.9 %copy-start.1 = (f32[16,4,448]{2,1,0:T(4,128)S(1)}, f32[16,4,448]{2,1,0:T(4,128)}, u32[]{:S(2)}) copy-start(f32[16,4,448]{2,1,0:T(4,128)} %latent_ref.1) | copy-start | bytes 344068
  2.0 0.7 %copy-start.3 = (f32[2,128]{1,0:T(2,128)S(1)}, f32[2,128]{1,0:T(2,128)}, u32[]{:S(2)}) copy-start(f32[2,128]{1,0:T(2,128)} %te_ref.1) | copy-start | bytes 3076
  2.6 0.7 %copy-start.4 = (f32[2]{0:T(128)S(1)}, f32[2]{0:T(128)}, u32[]{:S(2)}) copy-start(f32[2]{0:T(128)} %step_ref.1) | copy-start | bytes 28

commit v2 on v1

--- a/solution.py
+++ b/solution.py
@@ -8,6 +8,7 @@
 from jax.sharding import PartitionSpec as P
 
 ITERS = 3
+GROUP = 3
 LANES = 128
 MESH = pl.DeviceIdType.MESH
 
@@ -17,10 +18,10 @@
     step_ref, latent_ref, te_ref, cin_ref, cmid_ref, cout_ref,
     out_ref,
     win, wmid, wout, lat, low0, halo0, im, pre0, hid, ysum, mask,
-    table, bias, own, stage, halo, final, landed,
+    table, bias, own, stage, halo, final, landed, start,
     sem0_send, sem0_recv, tab_send, tab_recv, halo_send, halo_recv, fin_send, fin_recv,
 ):
-    sections, peers, per, total, chan, feat, rows, width, cols, margin, lanes = sizes
+    sections, peers, per, total, chan, feat, rows, width, cols, margin, lanes, group = sizes
     q, p = lax.axis_index("tm"), lax.axis_index("pix")
     evals = total - ITERS + 1
     edge = 3 * lanes
@@ -125,9 +126,11 @@
     for a in range(3):
         for b in range(3):
             t = 3 * a + b
-            win[:, t * chan : (t + 1) * chan] = cin_ref[a, b]
             wmid[:, t * feat : (t + 1) * feat] = cmid_ref[a, b]
             wout[t * chan : (t + 1) * chan, :] = cout_ref[a, b]
+
+    taps = jnp.concatenate([cin_ref[t // 3, t % 3] for t in range(9)], axis=0)
+    win[...] = taps.astype(jnp.float32).T.astype(jnp.bfloat16)
 
     col = lax.broadcasted_iota(jnp.int32, (8, lanes), 1) + (q * cols - margin)
     inside = jnp.where((col >= 0) & (col < width), 0.5, 0.0).astype(jnp.float32)
@@ -140,42 +143,37 @@
         h = v * m
         return h + h * jnp.tanh(h)
 
-    def spread(lows):
+    def spread(u, lows):
         for a in range(3):
             for b in range(3):
                 t = 3 * a + b
-                im[t * chan : (t + 1) * chan, :] = lows[b][:, a * lanes : (a + hid_rows) * lanes]
-
-    def first_layer(pre, j, h0, count):
+                im[u, t * chan : (t + 1) * chan, :] = lows[b][:, a * lanes : (a + hid_rows) * lanes]
+
+    def first_layer(u, pre, j, h0, count):
         te = bias[j]
         for i in range(count):
             h = h0 + i
             v = pre[:, i * lanes : (i + 1) * lanes] + te
             x = gated(v, mask[0:1, h * lanes : (h + 1) * lanes])
             span = slice(h * lanes, (h + 1) * lanes)
-            hid[0:feat, span] = pltpu.roll(x, 1, 1).astype(jnp.bfloat16)
-            hid[feat : 2 * feat, span] = x.astype(jnp.bfloat16)
-            hid[2 * feat :, span] = pltpu.roll(x, lanes - 1, 1).astype(jnp.bfloat16)
-
-    def rest(j):
-        w = wmid[...]
-        for s0 in range(0, sec_rows, 2):
-            n = min(2, sec_rows - s0)
-            x = jnp.concatenate(
-                [hid[:, (s0 + a) * lanes : (s0 + a + n) * lanes] for a in range(3)], axis=0
-            )
-            v = jnp.dot(w, x, preferred_element_type=jnp.float32)
-            m = mask[0:1, (s0 + 1) * lanes : (s0 + 1 + n) * lanes]
-            second = gated(v, m).astype(jnp.bfloat16)
-            ysum[:, s0 * lanes : (s0 + n) * lanes] = jnp.dot(
-                wout[...], second, preferred_element_type=jnp.float32
-            )
+            hid[u, 0:feat, span] = pltpu.roll(x, 1, 1).astype(jnp.bfloat16)
+            hid[u, feat : 2 * feat, span] = x.astype(jnp.bfloat16)
+            hid[u, 2 * feat :, span] = pltpu.roll(x, lanes - 1, 1).astype(jnp.bfloat16)
+
+    def second_layer(u, s0, n):
+        x = jnp.concatenate(
+            [hid[u, :, (s0 + a) * lanes : (s0 + a + n) * lanes] for a in range(3)], axis=0
+        )
+        v = jnp.dot(wmid[...], x, preferred_element_type=jnp.float32)
+        return gated(v, mask[0:1, (s0 + 1) * lanes : (s0 + 1 + n) * lanes]).astype(jnp.bfloat16)
+
+    def last_layer(u):
         parts = []
         for b in range(3):
             z = None
             for a in range(3):
                 t = 3 * a + b
-                y = ysum[t * chan : (t + 1) * chan, a * lanes : (a + rows) * lanes]
+                y = ysum[u, t * chan : (t + 1) * chan, a * lanes : (a + rows) * lanes]
                 z = y if z is None else z + y
             parts.append(z)
         return parts[1] + pltpu.roll(parts[0], 1, 1) + pltpu.roll(parts[2], rows * lanes - 1, 1)
@@ -188,83 +186,99 @@
     def _():
         first_copy(False).wait_recv()
 
-    spread([jnp.concatenate([halo0[0, b], low0[b], halo0[1, b]], axis=1) for b in range(3)])
+    spread(0, [jnp.concatenate([halo0[0, b], low0[b], halo0[1, b]], axis=1) for b in range(3)])
     for h0 in range(0, hid_rows, 2):
         n = min(2, hid_rows - h0)
         span = slice(h0 * lanes, (h0 + n) * lanes)
-        pre0[:, span] = jnp.dot(win[...], im[:, span], preferred_element_type=jnp.float32)
+        pre0[:, span] = jnp.dot(win[...], im[0, :, span], preferred_element_type=jnp.float32)
 
     for s in range(1, sections):
         table_copy(s).wait_recv()
     for j in range(total):
-        bias[j] = jnp.broadcast_to(table[j, 0:1, :], (feat, feat)).T
+        bias[j] = jnp.broadcast_to(table[j, 0:1, :], (lanes, feat)).T
 
     flat = jnp.concatenate([inside[0:1, :] * 2.0] * rows, axis=1)
 
-    def advance(k, j, summed):
-        slot = k * evals + j - k
-        if k == 0:
-            state = lat[...]
-            first_layer(pre0[...], j, 0, hid_rows)
-        else:
-            came = slot - evals
-
+    def advance(k, j0, summed):
+        slots = [k * evals + j0 + u - k for u in range(group)]
+        times = [j0 + u for u in range(group)]
+        if k:
             @pl.when(p < peers - 1)
             def _():
-                halo_copy(True, came).wait_recv()
+                for slot in slots:
+                    halo_copy(True, slot - evals).wait_recv()
 
             @pl.when(p > 0)
             def _():
-                halo_copy(False, came).wait_recv()
-
-            state = own[came]
-            centre = jnp.concatenate(
-                [halo[0, came].astype(jnp.float32), state, halo[1, came].astype(jnp.float32)], axis=1
-            )
-            span = low_rows * lanes
-            spread([
-                pltpu.roll(centre, 1, 1).astype(jnp.bfloat16),
-                centre.astype(jnp.bfloat16),
-                pltpu.roll(centre, span - 1, 1).astype(jnp.bfloat16),
-            ])
-            for h0 in range(0, hid_rows, 2):
-                n = min(2, hid_rows - h0)
-                pre = jnp.dot(
-                    win[...], im[:, h0 * lanes : (h0 + n) * lanes], preferred_element_type=jnp.float32
+                for slot in slots:
+                    halo_copy(False, slot - evals).wait_recv()
+
+            for u, slot in enumerate(slots):
+                came = slot - evals
+                centre = jnp.concatenate(
+                    [halo[0, came].astype(jnp.float32), own[came], halo[1, came].astype(jnp.float32)],
+                    axis=1,
                 )
-                first_layer(pre, j, h0, n)
-        output = state + rest(j)
-        step = table[j, 1:2, :]
-        summed = summed + jnp.concatenate([step] * rows, axis=1) * output
-        reached = lat[...] + summed
+                spread(u, [
+                    pltpu.roll(centre, 1, 1).astype(jnp.bfloat16),
+                    centre.astype(jnp.bfloat16),
+                    pltpu.roll(centre, low_rows * lanes - 1, 1).astype(jnp.bfloat16),
+                ])
+        for h0 in range(0, hid_rows, 2):
+            n = min(2, hid_rows - h0)
+            span = slice(h0 * lanes, (h0 + n) * lanes)
+            for u in range(group):
+                if k:
+                    pre = jnp.dot(win[...], im[u, :, span], preferred_element_type=jnp.float32)
+                else:
+                    pre = pre0[:, span]
+                first_layer(u, pre, times[u], h0, n)
+        for s0 in range(0, sec_rows, 2):
+            n = min(2, sec_rows - s0)
+            seconds = [second_layer(u, s0, n) for u in range(group)]
+            for u in range(group):
+                ysum[u, :, s0 * lanes : (s0 + n) * lanes] = jnp.dot(
+                    wout[...], seconds[u], preferred_element_type=jnp.float32
+                )
+        for u in range(group):
+            state = own[slots[u] - evals] if k else lat[...]
+            step = table[times[u], 1:2, :]
+            summed = summed + jnp.concatenate([step] * rows, axis=1) * (state + last_layer(u))
+            reached = lat[...] + summed
+            if k < ITERS - 1:
+                reached = reached * flat
+                own[slots[u]] = reached
+                stage[slots[u]] = reached.astype(jnp.bfloat16)
+                if u == 0:
+                    @pl.when(j0 == k)
+                    def _(summed=summed):
+                        start[...] = summed
+            else:
+                final[times[u]] = reached
         if k < ITERS - 1:
-            reached = reached * flat
-            own[slot] = reached
-            stage[slot] = reached.astype(jnp.bfloat16)
-
             @pl.when(p > 0)
             def _():
-                halo_copy(True, slot).start()
+                for slot in slots:
+                    halo_copy(True, slot).start()
 
             @pl.when(p < peers - 1)
             def _():
-                halo_copy(False, slot).start()
+                for slot in slots:
+                    halo_copy(False, slot).start()
         else:
-            final[j] = reached
-            deliver(final.at[j], j)
+            for j in times:
+                deliver(final.at[j], j)
         return summed
 
-    start = jnp.zeros((chan, rows * lanes), jnp.float32)
+    start[...] = jnp.zeros_like(start)
     for k in range(ITERS):
-        first = advance(k, jnp.int32(k), start)
+
+        def body(i, summed, k=k):
+            return advance(k, k + i * group, summed)
+
+        lax.fori_loop(0, evals // group, body, start[...])
         if k < ITERS - 1:
-            deliver(own.at[k * evals], k)
-
-        def body(j, summed, k=k):
-            return advance(k, j, summed)
-
-        lax.fori_loop(k + 1, k + evals, body, first)
-        start = first
+            deliver(own.at[k * evals], jnp.int32(k))
 
     for s in range(1, sections):
         table_copy(s).wait_send()
@@ -324,7 +338,8 @@
     lanes = (cols + 2 * margin + LANES - 1) // LANES * LANES
     evals = total - ITERS + 1
     slots = (ITERS - 1) * evals
-    sizes = (sections, peers, per, total, chan, feat, rows, width, cols, margin, lanes)
+    group = next(g for g in (GROUP, 2, 1) if evals % g == 0)
+    sizes = (sections, peers, per, total, chan, feat, rows, width, cols, margin, lanes, group)
     vmem = pl.BlockSpec(memory_space=pltpu.VMEM)
     f32, bf16 = jnp.float32, jnp.bfloat16
     dma = pltpu.SemaphoreType.DMA
@@ -340,18 +355,19 @@
             pltpu.VMEM((chan, rows * lanes), f32),
             pltpu.VMEM((3, chan, rows * lanes), bf16),
             pltpu.VMEM((2, 3, chan, 3 * lanes), bf16),
-            pltpu.VMEM((9 * chan, (rows + 4) * lanes), bf16),
+            pltpu.VMEM((group, 9 * chan, (rows + 4) * lanes), bf16),
             pltpu.VMEM((feat, (rows + 4) * lanes), f32),
-            pltpu.VMEM((3 * feat, (rows + 4) * lanes), bf16),
-            pltpu.VMEM((9 * chan, (rows + 2) * lanes), f32),
+            pltpu.VMEM((group, 3 * feat, (rows + 4) * lanes), bf16),
+            pltpu.VMEM((group, 9 * chan, (rows + 2) * lanes), f32),
             pltpu.VMEM((8, (rows + 4) * lanes), f32),
             pltpu.VMEM((total, 8, feat), f32),
-            pltpu.VMEM((total, feat, feat), f32),
+            pltpu.VMEM((total, feat, lanes), f32),
             pltpu.VMEM((slots, chan, rows * lanes), f32),
             pltpu.VMEM((slots, chan, rows * lanes), bf16),
             pltpu.VMEM((2, slots, chan, 3 * lanes), bf16),
             pltpu.VMEM((total, chan, rows * lanes), f32),
             pltpu.VMEM((sections, per, chan, rows * lanes), f32),
+            pltpu.VMEM((chan, rows * lanes), f32),
             dma((2,)), dma((2,)),
             dma((sections - 1,)), dma((sections - 1,)),
             dma((2, slots)), dma((2, slots)),
@@ -360,7 +376,7 @@
         compiler_params=pltpu.CompilerParams(
             collective_id=0, has_side_effects=True, vmem_limit_bytes=40 * 1024 * 1024
         ),
-    )(step_size, latent, time_embed, conv_in, conv_mid, conv_out)
+    )(step_size, latent, time_embed, jnp.swapaxes(conv_in, 2, 3), conv_mid, conv_out)
     return jnp.transpose(out, (0, 2, 1, 3))
 
 

time: 39.1 us -> 31 us (0.79)
  Pallas kernels: 34.4 us -> 25.8 us
  local copies, waits for them, and re-layouts: 4.14 us -> 4.95 us
    pallas_call x1, Pallas kernels: 34.4 us -> 25.8 us  [shards(): pl.pallas_call(functools.partial(kernel, sizes), out_shape=jax.ShapeDtype...]
    unnamed x11 -> x12, local copies, waits for them, and re-layouts: 3.27 us -> 4.08 us
where the time goes in v2:
time: 31 us; the launch traced here: 30.7 us
  Pallas kernels  25.8 us (83%)
  local copies, waits for them, and re-layouts  4.95 us (16%)
    pallas_call x1, Pallas kernels, shards(): pl.pallas_call(functools.partial(kernel, sizes), out_shape=jax.ShapeDtype...  25.8 us
    unnamed x12, local copies, waits for them, and re-layouts  4.08 us
    transpose x1, local copies, waits for them, and re-layouts, shards(): return jnp.transpose(out, (0, 2, 1, 3))  0.87 us

profile of v2, /device:TPU:15, one launch (start us, length us, event | category | flops | bytes accessed | tf_op | source)
XLA Modules:
  0.0 30.7 jit_solution(11890497940600188587)
XLA Ops:
  0.0 0.0 copy-start.4
  0.0 0.0 copy-start.5
  0.0 0.7 %copy-done.4 = f32[2,128]{1,0:T(2,128)S(1)} copy-done((f32[2,128]{1,0:T(2,128)S(1)}, f32[2,128]{1,0:T(2,128)}, u32[]{:S(2)}) %copy-start.4) | copy-done | bytes 1048
  0.7 0.0 copy-done.5
  0.7 0.0 copy-start
  0.7 1.0 %copy-done = bf16[3,3,128,128]{3,2,1,0:T(8,128)(2,1)S(1)} copy-done((bf16[3,3,128,128]{3,2,1,0:T(8,128)(2,1)S(1)}, bf16[3,3,128,128]{3,2,1,0:T(8,128)(2,1)}, u32[]{:S(2)}) %copy-start) | copy-done | bytes 294936
  1.6 0.0 copy-start.1
  1.6 0.9 %copy-done.1 = f32[16,4,448]{2,1,0:T(4,128)S(1)} copy-done((f32[16,4,448]{2,1,0:T(4,128)S(1)}, f32[16,4,448]{2,1,0:T(4,128)}, u32[]{:S(2)}) %copy-start.1) | copy-done | bytes 114712
  2.5 0.0 copy-start.2
  2.6 0.8 %copy-done.2 = bf16[3,3,128,16]{2,3,1,0:T(8,128)(2,1)S(1)} copy-done((bf16[3,3,128,16]{2,3,1,0:T(8,128)(2,1)S(1)}, bf16[3,3,128,16]{2,3,1,0:T(8,128)(2,1)}, u32[]{:S(2)}) %copy-start.2) | copy-done | bytes 36888
  3.3 0.0 copy-start.3
  3.3 0.8 %copy-done.3 = bf16[3,3,16,128]{3,2,1,0:T(8,128)(2,1)S(1)} copy-done((bf16[3,3,16,128]{3,2,1,0:T(8,128)(2,1)S(1)}, bf16[3,3,16,128]{3,2,1,0:T(8,128)(2,1)}, u32[]{:S(2)}) %copy-start.3) | copy-done | bytes 36888
  4.1 25.8 %shard_map.64 = f32[2,4,16,448]{3,2,1,0:T(8,128)S(1)} custom-call(f32[2]{0:T(128)S(1)} %copy-done.5, f32[16,4,448]{2,1,0:T(4,128)S(1)} %copy-done.1, f32[2,128]{1,0:T(2,128)S(1)} %copy-done.4, bf16[3,3,16,128]{3,2,1,0:T(8,128)(2,1)S(1)} %bitcast.3, bf16[3,3,128,128]{3,2,1,0:T(8,128)(2,1)S(1)} %copy-done, bf16[3,3,16,128]{3,2,1,0:T(8,128)(2,1)S(1)} %copy-done.3), custom_call_target="tpu_custom_call" | custom-call | tf_op jit(solution)/shard_map/pallas_call | solution.py:346
  29.9 0.9 %copy.7 = f32[2,16,4,448]{3,2,1,0:T(4,128)} copy(f32[2,16,4,448]{3,1,2,0:T(8,128)S(1)} %bitcast.2) | data formatting | bytes 458752 | tf_op jit(solution)/shard_map/transpose | solution.py:380
Async XLA Ops:
  0.0 0.7 %copy-start.4 = (f32[2,128]{1,0:T(2,128)S(1)}, f32[2,128]{1,0:T(2,128)}, u32[]{:S(2)}) copy-start(f32[2,128]{1,0:T(2,128)} %te_ref.1) | copy-start | bytes 3076
  0.0 0.7 %copy-start.5 = (f32[2]{0:T(128)S(1)}, f32[2]{0:T(128)}, u32[]{:S(2)}) copy-start(f32[2]{0:T(128)} %step_ref.1) | copy-start | bytes 28
  0.7 1.0 %copy-start = (bf16[3,3,128,128]{3,2,1,0:T(8,128)(2,1)S(1)}, bf16[3,3,128,128]{3,2,1,0:T(8,128)(2,1)}, u32[]{:S(2)}) copy-start(bf16[3,3,128,128]{3,2,1,0:T(8,128)(2,1)} %cmid_ref.1) | copy-start | bytes 884740
  1.6 0.9 %copy-start.1 = (f32[16,4,448]{2,1,0:T(4,128)S(1)}, f32[16,4,448]{2,1,0:T(4,128)}, u32[]{:S(2)}) copy-start(f32[16,4,448]{2,1,0:T(4,128)} %latent_ref.1) | copy-start | bytes 344068
  2.5 0.8 %copy-start.2 = (bf16[3,3,128,16]{2,3,1,0:T(8,128)(2,1)S(1)}, bf16[3,3,128,16]{2,3,1,0:T(8,128)(2,1)}, u32[]{:S(2)}) copy-start(bf16[3,3,128,16]{2,3,1,0:T(8,128)(2,1)} %param.9) | copy-start | bytes 110596
  3.3 0.8 %copy-start.3 = (bf16[3,3,16,128]{3,2,1,0:T(8,128)(2,1)S(1)}, bf16[3,3,16,128]{3,2,1,0:T(8,128)(2,1)}, u32[]{:S(2)}) copy-start(bf16[3,3,16,128]{3,2,1,0:T(8,128)(2,1)} %cout_ref.1) | copy-start | bytes 110596

commit v3 on v2

--- a/solution.py
+++ b/solution.py
@@ -15,10 +15,11 @@
 
 def kernel(
     sizes,
-    step_ref, latent_ref, te_ref, cin_ref, cmid_ref, cout_ref,
+    step_hbm, latent_hbm, te_hbm, cin_hbm, cmid_hbm, cout_hbm,
     out_ref,
     win, wmid, wout, lat, low0, halo0, im, pre0, hid, ysum, mask,
     table, bias, own, stage, halo, final, landed, start,
+    step_ref, latent_ref, te_ref, cin_ref, cmid_ref, cout_ref, load_sem,
     sem0_send, sem0_recv, tab_send, tab_recv, halo_send, halo_recv, fin_send, fin_recv,
 ):
     sections, peers, per, total, chan, feat, rows, width, cols, margin, lanes, group = sizes
@@ -27,6 +28,16 @@
     edge = 3 * lanes
     hid_rows, sec_rows, low_rows = rows + 4, rows + 2, rows + 6
 
+    loads = [
+        pltpu.make_async_copy(source, target, load_sem.at[i])
+        for i, (source, target) in enumerate([
+            (latent_hbm, latent_ref), (te_hbm, te_ref), (step_hbm, step_ref),
+            (cin_hbm, cin_ref), (cmid_hbm, cmid_ref), (cout_hbm, cout_ref),
+        ])
+    ]
+    for load in loads:
+        load.start()
+
     barrier = pltpu.get_barrier_semaphore()
     for s in range(1, sections):
         pl.semaphore_signal(barrier, inc=1, device_id=(lax.rem(q + s, sections), p), device_id_type=MESH)
@@ -38,6 +49,9 @@
     @pl.when(p < peers - 1)
     def _():
         pl.semaphore_signal(barrier, inc=1, device_id=(q, p + 1), device_id_type=MESH)
+
+    for load in loads[:3]:
+        load.wait()
 
     for j in range(per):
         table[q * per + j] = jnp.concatenate(
@@ -123,6 +137,9 @@
     for s in range(1, sections):
         table_copy(s).start()
 
+    for load in loads[3:]:
+        load.wait()
+
     for a in range(3):
         for b in range(3):
             t = 3 * a + b
@@ -154,11 +171,11 @@
         for i in range(count):
             h = h0 + i
             v = pre[:, i * lanes : (i + 1) * lanes] + te
-            x = gated(v, mask[0:1, h * lanes : (h + 1) * lanes])
+            x = gated(v, mask[0:1, h * lanes : (h + 1) * lanes]).astype(jnp.bfloat16)
             span = slice(h * lanes, (h + 1) * lanes)
-            hid[u, 0:feat, span] = pltpu.roll(x, 1, 1).astype(jnp.bfloat16)
-            hid[u, feat : 2 * feat, span] = x.astype(jnp.bfloat16)
-            hid[u, 2 * feat :, span] = pltpu.roll(x, lanes - 1, 1).astype(jnp.bfloat16)
+            hid[u, 0:feat, span] = pltpu.roll(x, 1, 1)
+            hid[u, feat : 2 * feat, span] = x
+            hid[u, 2 * feat :, span] = pltpu.roll(x, lanes - 1, 1)
 
     def second_layer(u, s0, n):
         x = jnp.concatenate(
@@ -233,13 +250,15 @@
                 else:
                     pre = pre0[:, span]
                 first_layer(u, pre, times[u], h0, n)
-        for s0 in range(0, sec_rows, 2):
+        ready = []
+        for s0 in [*range(0, sec_rows, 2), sec_rows]:
             n = min(2, sec_rows - s0)
-            seconds = [second_layer(u, s0, n) for u in range(group)]
-            for u in range(group):
-                ysum[u, :, s0 * lanes : (s0 + n) * lanes] = jnp.dot(
-                    wout[...], seconds[u], preferred_element_type=jnp.float32
+            fresh = [(u, s0, n, second_layer(u, s0, n)) for u in range(group if n else 0)]
+            for u, r0, m, second in ready:
+                ysum[u, :, r0 * lanes : (r0 + m) * lanes] = jnp.dot(
+                    wout[...], second, preferred_element_type=jnp.float32
                 )
+            ready = fresh
         for u in range(group):
             state = own[slots[u] - evals] if k else lat[...]
             step = table[times[u], 1:2, :]
@@ -346,7 +365,7 @@
     out = pl.pallas_call(
         functools.partial(kernel, sizes),
         out_shape=jax.ShapeDtypeStruct((per, rows, chan, width), f32),
-        in_specs=[pl.BlockSpec(memory_space=pltpu.SMEM)] + [vmem] * 5,
+        in_specs=[pl.BlockSpec(memory_space=pltpu.HBM)] * 6,
         out_specs=vmem,
         scratch_shapes=[
             pltpu.VMEM((feat, 9 * chan), bf16),
@@ -368,13 +387,20 @@
             pltpu.VMEM((total, chan, rows * lanes), f32),
             pltpu.VMEM((sections, per, chan, rows * lanes), f32),
             pltpu.VMEM((chan, rows * lanes), f32),
+            pltpu.SMEM(step_size.shape, f32),
+            pltpu.VMEM(latent.shape, f32),
+            pltpu.VMEM(time_embed.shape, f32),
+            pltpu.VMEM((3, 3, chan, feat), bf16),
+            pltpu.VMEM(conv_mid.shape, bf16),
+            pltpu.VMEM(conv_out.shape, bf16),
+            dma((6,)),
             dma((2,)), dma((2,)),
             dma((sections - 1,)), dma((sections - 1,)),
             dma((2, slots)), dma((2, slots)),
             dma((total,)), dma((sections, per)),
         ],
         compiler_params=pltpu.CompilerParams(
-            collective_id=0, has_side_effects=True, vmem_limit_bytes=40 * 1024 * 1024
+            collective_id=0, has_side_effects=True, vmem_limit_bytes=60 * 1024 * 1024
         ),
     )(step_size, latent, time_embed, jnp.swapaxes(conv_in, 2, 3), conv_mid, conv_out)
     return jnp.transpose(out, (0, 2, 1, 3))

time: 31 us -> 26.1 us (0.84)
  local copies, waits for them, and re-layouts: 4.95 us -> 1.82 us
  Pallas kernels: 25.8 us -> 24.1 us
    unnamed x12 -> x0, local copies, waits for them, and re-layouts: 4.08 us -> none
    pallas_call x1, Pallas kernels: 25.8 us -> 24.1 us  [shards(): pl.pallas_call(functools.partial(kernel, sizes), out_shape=jax.ShapeDtype...]
    transpose x1, local copies, waits for them, and re-layouts: 0.87 us -> 1.82 us  [shards(): return jnp.transpose(out, (0, 2, 1, 3))]
where the time goes in v3:
time: 26.1 us; the launch traced here: 25.9 us
  Pallas kernels  24.1 us (92%)
  local copies, waits for them, and re-layouts  1.82 us (7%)
    pallas_call x1, Pallas kernels, shards(): pl.pallas_call(functools.partial(kernel, sizes), out_shape=jax.ShapeDtype...  24.1 us
    transpose x1, local copies, waits for them, and re-layouts, shards(): return jnp.transpose(out, (0, 2, 1, 3))  1.82 us

profile of v3, /device:TPU:15, one launch (start us, length us, event | category | flops | bytes accessed | tf_op | source)
XLA Modules:
  0.0 25.9 jit_solution(15864886670407071801)
XLA Ops:
  0.0 24.1 %shard_map.64 = f32[2,4,16,448]{3,2,1,0:T(8,128)} custom-call(f32[2]{0:T(128)} %step_hbm.1, f32[16,4,448]{2,1,0:T(4,128)} %latent_hbm.1, f32[2,128]{1,0:T(2,128)} %te_hbm.1, bf16[3,3,16,128]{3,2,1,0:T(8,128)(2,1)} %bitcast.3, bf16[3,3,128,128]{3,2,1,0:T(8,128)(2,1)} %cmid_hbm.1, bf16[3,3,16,128]{3,2,1,0:T(8,128)(2,1)} %cout_hbm.1), custom_call_target="tpu_custom_call" | custom-call | tf_op jit(solution)/shard_map/pallas_call | solution.py:365
  24.1 1.8 %copy.7 = f32[2,16,4,448]{3,2,1,0:T(4,128)} copy(f32[2,16,4,448]{3,1,2,0:T(8,128)} %bitcast.2) | data formatting | bytes 458752 | tf_op jit(solution)/shard_map/transpose | solution.py:406

commit v4 on v3

--- a/solution.py
+++ b/solution.py
@@ -233,13 +233,13 @@
             for u, slot in enumerate(slots):
                 came = slot - evals
                 centre = jnp.concatenate(
-                    [halo[0, came].astype(jnp.float32), own[came], halo[1, came].astype(jnp.float32)],
+                    [halo[0, came], stage[came], halo[1, came]],
                     axis=1,
                 )
                 spread(u, [
-                    pltpu.roll(centre, 1, 1).astype(jnp.bfloat16),
-                    centre.astype(jnp.bfloat16),
-                    pltpu.roll(centre, low_rows * lanes - 1, 1).astype(jnp.bfloat16),
+                    pltpu.roll(centre, 1, 1),
+                    centre,
+                    pltpu.roll(centre, low_rows * lanes - 1, 1),
                 ])
         for h0 in range(0, hid_rows, 2):
             n = min(2, hid_rows - h0)

time: 26.1 us -> 26.1 us (level)
  no operation moved by 1% of the time
where the time goes in v4:
time: 26.1 us; the launch traced here: 25.9 us
  Pallas kernels  24.1 us (92%)
  local copies, waits for them, and re-layouts  1.82 us (7%)
    pallas_call x1, Pallas kernels, shards(): pl.pallas_call(functools.partial(kernel, sizes), out_shape=jax.ShapeDtype...  24.1 us
    transpose x1, local copies, waits for them, and re-layouts, shards(): return jnp.transpose(out, (0, 2, 1, 3))  1.82 us

profile of v4, /device:TPU:15, one launch (start us, length us, event | category | flops | bytes accessed | tf_op | source)
XLA Modules:
  0.0 25.9 jit_solution(1012538081918233554)
XLA Ops:
  0.0 24.1 %shard_map.64 = f32[2,4,16,448]{3,2,1,0:T(8,128)} custom-call(f32[2]{0:T(128)} %step_hbm.1, f32[16,4,448]{2,1,0:T(4,128)} %latent_hbm.1, f32[2,128]{1,0:T(2,128)} %te_hbm.1, bf16[3,3,16,128]{3,2,1,0:T(8,128)(2,1)} %bitcast.3, bf16[3,3,128,128]{3,2,1,0:T(8,128)(2,1)} %cmid_hbm.1, bf16[3,3,16,128]{3,2,1,0:T(8,128)(2,1)} %cout_hbm.1), custom_call_target="tpu_custom_call" | custom-call | tf_op jit(solution)/shard_map/pallas_call | solution.py:365
  24.1 1.8 %copy.7 = f32[2,16,4,448]{3,2,1,0:T(4,128)} copy(f32[2,16,4,448]{3,1,2,0:T(8,128)} %bitcast.2) | data formatting | bytes 458752 | tf_op jit(solution)/shard_map/transpose | solution.py:406
